TPU v7x, 32 devices: a whole 2x2x4 slice. The times are simulated.
32 devices in a mesh: view: 4 (over y, x), depth: 8 (over z, core).
Axes of the slice: x: 2, y: 2, z: 4, core: 2. Of those that a mesh axis runs over, the one named last changes fastest.
Arguments:
- estimate: float32 [64, 128, 256], P('depth', 'view'), may hold values from 0.5 to 2
- observed: float32 [8, 64, 128, 256], P('view', 'depth'), may hold values from 0.05 to 30, as said below
- voxel_weights: bfloat16 [8, 8, 64, 128, 256], P('view', None, 'depth'), may hold values from 0.029907227 to 0.29882812
- lateral_taps: float32 [8, 8, 2, 9], P('view'), may hold values from 0.05 to 1
- axial_taps: float32 [8, 9], P('view'), may hold values from 0.05 to 1
Outputs:
- updated: float32 [64, 128, 256], P('depth', 'view')
- divergence: float32 [8], P('view')
Inputs may be any that keep to these rules, and one draw needn't show every extreme that they name: `observed`: strictly positive.
All inputs are finite; a program needn't handle non-finite values.
Results may differ from a plain program's by a relative error of at most 0.0003.
Values sent between devices are 32-bit elements; how exact they have to be, the bound alone decides.
No kernel may reach another device: no remote copies, remote signals or barrier semaphores. Data moves between devices by JAX's collectives and lax.ppermute only.
A program may use at most 128 MiB of HBM per device.

v0:
```python
import jax
import jax.numpy as jnp
from jax import lax
from jax.experimental import pallas as pl
from jax.experimental.pallas import tpu as pltpu
from jax.sharding import PartitionSpec as P

TAPS = 9
RADIUS = 4
ITERS = 2
F32 = jnp.float32
BF16 = jnp.bfloat16
NOISE_SHIFTS = 64


def mxu(left, right):
    return jnp.dot(left, right, preferred_element_type=F32)


def noise_rows(bases, height):
    return bases * height + 8 * NOISE_SHIFTS


def noise_at(place_ref, view, z, rows):
    shift = lax.rem(37 * (place_ref[1] + view) + 11 * (place_ref[2] + z), NOISE_SHIFTS)
    return pl.ds(pl.multiple_of(shift * 8, 8), rows)


def prepare_kernel(taps_ref, lateral_ref, axial_ref, x_ref, xt_ref, y_ref, yt_ref, axial_out_ref, noise_ref, gain_ref):
    view = pl.program_id(0)
    bases, breadth, height = x_ref.shape[1], x_ref.shape[2], yt_ref.shape[1]
    tall, wide = 32, 128
    inverses = []
    for base in range(bases):
        taps = lateral_ref[0, base]
        inverse = 1.0 / jnp.sum(taps, axis=-1, keepdims=True)
        sums = jnp.sum((taps * inverse).astype(BF16).astype(F32), axis=-1, keepdims=True)
        gain = 1.0 / (sums[0:1] * sums[1:2])
        gain_ref[0, base : base + 1, :] = jnp.broadcast_to(gain, (1, gain_ref.shape[2]))
        inverses.append([jnp.broadcast_to(inverse[k : k + 1], (tall, wide)) for k in range(2)])

    def banded(masks, base, kind, sign):
        total = jnp.zeros((tall, wide), F32)
        for tap in range(TAPS):
            total = jnp.where(masks[tap if sign > 0 else TAPS - 1 - tap], taps_ref[view, base, kind, tap], total)
        return (total * inverses[base][kind]).astype(BF16)

    for r in range(0, breadth, tall):
        for c in range(0, breadth, wide):
            at = (slice(r, r + tall), slice(c, c + wide))
            lateral = r < height and c < height
            if r + tall + RADIUS <= c or c + wide + RADIUS <= r:
                empty = jnp.zeros((tall, wide), BF16)
                for base in range(bases):
                    x_ref[(0, base) + at] = empty
                    xt_ref[(0, base) + at] = empty
                    if lateral:
                        y_ref[0, base * height + r : base * height + r + tall, at[1]] = empty
                        yt_ref[0, at[0], base * height + c : base * height + c + wide] = empty
                continue
            rows = lax.broadcasted_iota(jnp.int32, (tall, wide), 0) + r
            columns = lax.broadcasted_iota(jnp.int32, (tall, wide), 1) + c
            masks = [rows - columns + RADIUS == tap for tap in range(TAPS)]
            for base in range(bases):
                x_ref[(0, base) + at] = banded(masks, base, 1, 1)
                xt_ref[(0, base) + at] = banded(masks, base, 1, -1)
                if lateral:
                    y_ref[0, base * height + r : base * height + r + tall, at[1]] = banded(masks, base, 0, -1)
                    yt_ref[0, at[0], base * height + c : base * height + c + wide] = banded(masks, base, 0, 1)

    @pl.when(pl.program_id(0) == 0)
    def _():
        axial = axial_ref[...]
        axial_out_ref[...] = axial / jnp.sum(axial, axis=-1, keepdims=True)

        def fill(k, carry):
            first = pl.multiple_of(k * 64, 64)
            rows = lax.broadcasted_iota(jnp.int32, (64, breadth), 0) + first
            columns = lax.broadcasted_iota(jnp.int32, (64, breadth), 1)
            mixed = rows * 1664525 + columns * 22695477 + 12345
            for odd, shift in ((739982445, 15), (695872825, 12)):
                mixed = (mixed ^ lax.shift_right_logical(mixed, shift)) * odd
            mixed = mixed ^ lax.shift_right_logical(mixed, 15)
            both = (mixed & 2047) + (lax.shift_right_logical(mixed, 16) & 2047)
            noise_ref[pl.ds(first, 64), :] = 1.0 + (both - 2047).astype(F32) * (1.0 / (2048 * 128))
            return carry

        lax.fori_loop(0, noise_ref.shape[0] // 64, fill, 0)


def adjoint_half(weigh, xt, yt_ref, field_ref, mixed):
    half, rows, _ = mixed.shape
    height = yt_ref.shape[0]
    bases = rows // (2 * height)
    for base in range(bases):
        swept = mxu(weigh(base), xt[base])
        high = swept.astype(BF16)
        low = (swept - high.astype(F32)).astype(BF16)
        for z in range(half):
            at = slice(z * height, (z + 1) * height)
            mixed[z, base * height : (base + 1) * height, :] = high[at]
            mixed[z, (bases + base) * height : (bases + base + 1) * height, :] = low[at]
    twice = jnp.concatenate([yt_ref[...], yt_ref[...]], axis=1)
    for z in range(half):
        field_ref[0, z] = mxu(twice, mixed[z])


def ones_kernel(place_ref, weights_any, xt_any, yt_any, after_any, field_ref, weights, xt, yt, sems, mixed):
    view = pl.program_id(0)
    views, bases, half, height, breadth = weights.shape
    planes = pl.ds(place_ref[0] * half, half)

    def copies(at):
        pairs = ((weights_any.at[at, :, planes], weights), (xt_any.at[at], xt), (yt_any.at[at], yt))
        return [pltpu.make_async_copy(a, b.at[at], sems.at[at, k]) for k, (a, b) in enumerate(pairs)]

    @pl.when(view == 0)
    def _():
        for at in range(views):
            for copy in copies(at):
                copy.start()

    for copy in copies(view):
        copy.wait()
    adjoint_half(lambda base: weights[view, base].reshape(half * height, breadth), xt.at[view], yt.at[view], field_ref, mixed)


def step_kernel(place_ref, axial_ref, halo_ref, near_ref, far_ref, noise_ref, gain_ref, y_ref, counts_any, weights_any,
                x_any, xt_any, yt_any, after_any, field_ref, fidelity_ref, weights, counts_buf, x, xt, yt, sems,
                blurred, rows, mixed):
    view = pl.program_id(0)
    views, bases, half, height, breadth = weights.shape
    quarters, _, span, _ = near_ref.shape
    planes = pl.ds(place_ref[0] * half, half)

    def copies(at):
        pairs = ((x_any.at[at], x), (weights_any.at[at, :, planes], weights), (counts_any.at[at, planes], counts_buf),
                 (xt_any.at[at], xt), (yt_any.at[at], yt))
        return [pltpu.make_async_copy(a, b.at[at], sems.at[at, k]) for k, (a, b) in enumerate(pairs)]

    @pl.when(view == 0)
    def _():
        for at in range(views):
            for copy in copies(at):
                copy.start()

    def depth_blur(groups):
        for z in range(half):
            for q in range(quarters):
                total = None
                for tap in range(TAPS):
                    plane = z + tap
                    term = axial_ref[view, tap] * groups[plane // half][q, plane % half]
                    total = term if total is None else total + term
                high = total.astype(BF16)
                blurred[z, q * span : (q + 1) * span, :] = high
                blurred[z, height + q * span : height + (q + 1) * span, :] = (total - high.astype(F32)).astype(BF16)

    @pl.when(place_ref[0] == 0)
    def _():
        depth_blur((halo_ref, near_ref, far_ref))

    @pl.when(place_ref[0] != 0)
    def _():
        depth_blur((far_ref, near_ref, halo_ref))

    for copy in copies(view):
        copy.wait()
    twice = jnp.concatenate([y_ref[0], y_ref[0]], axis=1)
    for z in range(half):
        swept = mxu(twice, blurred[z]) * noise_ref[noise_at(place_ref, view, z, bases * height), :]
        for base in range(bases):
            gain = gain_ref[0, base : base + 1, :]
            rows[base, z * height : (z + 1) * height, :] = (swept[base * height : (base + 1) * height] * gain).astype(BF16)

    def weights_of(base):
        return weights[view, base].reshape(half * height, breadth).astype(F32)

    predicted = None
    for base in range(bases):
        term = weights_of(base) * mxu(rows[base], x[view, base])
        predicted = term if predicted is None else predicted + term
    counts = counts_buf[view].reshape(half * height, breadth)
    ratios = counts / predicted
    if fidelity_ref is not None:
        terms = counts * jnp.log(ratios) - counts + predicted
        fidelity_ref[0] = jnp.sum(terms.reshape(-1, 8, breadth), axis=0)
    noise = [noise_ref[noise_at(place_ref, view, z, height), :] for z in range(half)]
    spread = ratios * jnp.concatenate(noise, axis=0)
    adjoint_half(lambda base: (weights_of(base) * spread).astype(BF16), xt.at[view], yt.at[view], field_ref, mixed)


def plain_step_kernel(*refs):
    step_kernel(*refs[:15], None, *refs[15:])


def depth_adjoint(place_ref, axial_ref, groups, scale_ref, out_ref):
    views, half = groups[1].shape[:2]
    quarters, _, span, _ = out_ref.shape

    def run(ordered):
        def quarter(q, carry):
            at = pl.ds(pl.multiple_of(q * span, span), span)
            for z in range(half):
                product = None
                for view in range(views):
                    total = None
                    for tap in range(TAPS):
                        plane = z + 2 * RADIUS - tap
                        term = axial_ref[view, tap] * ordered[plane // half][view, plane % half, at, :]
                        total = term if total is None else total + term
                    product = total if product is None else product * total
                out_ref[q, z] = 1.0 / product if scale_ref is None else jnp.log(product * scale_ref[q, z])
            return carry

        lax.fori_loop(0, quarters, quarter, 0)

    halo_ref, near_ref, far_ref = groups

    @pl.when(place_ref[0] == 0)
    def _():
        run((halo_ref, near_ref, far_ref))

    @pl.when(place_ref[0] != 0)
    def _():
        run((far_ref, near_ref, halo_ref))


def scale_kernel(place_ref, axial_ref, halo_ref, near_ref, far_ref, after_any, out_ref):
    depth_adjoint(place_ref, axial_ref, (halo_ref, near_ref, far_ref), None, out_ref)


def log_kernel(place_ref, axial_ref, halo_ref, near_ref, far_ref, scale_ref, after_any, out_ref):
    depth_adjoint(place_ref, axial_ref, (halo_ref, near_ref, far_ref), scale_ref, out_ref)


def share_kernel(place_ref, own_ref, copies_ref, current_ref):
    current_ref[...] = own_ref[0]
    for q in range(copies_ref.shape[0]):
        copies_ref[q] = own_ref[0]


def corrected(pieces_ref, current_ref, views_total):
    total = pieces_ref[0]
    for q in range(1, pieces_ref.shape[0]):
        total = total + pieces_ref[q]
    return current_ref[...] * jnp.exp(total * (1.0 / views_total))


def whole(shape):
    return pl.BlockSpec(shape, lambda *_: (0,) * len(shape))


def per_view(shape):
    return pl.BlockSpec((1,) + shape[1:], lambda v, *_: (v,) + (0,) * (len(shape) - 1))


ANY = pl.BlockSpec(memory_space=pl.ANY)
SMEM = pl.BlockSpec(memory_space=pltpu.SMEM)


def call(kernel, grid, in_specs, out_shape, out_specs, scratch=(), prefetch=1, cost=(0, 0), vmem=16, **more):
    return pl.pallas_call(
        kernel,
        out_shape=out_shape,
        grid_spec=pltpu.PrefetchScalarGridSpec(
            num_scalar_prefetch=prefetch, grid=grid, in_specs=in_specs, out_specs=out_specs, scratch_shapes=list(scratch)),
        compiler_params=pltpu.CompilerParams(vmem_limit_bytes=vmem * 1024 * 1024),
        cost_estimate=pl.CostEstimate(flops=cost[0], bytes_accessed=cost[1], transcendentals=0),
        **more,
    )


def body(estimate, observed, voxel_weights, lateral_taps, axial_taps):
    views, planes, height, breadth = observed.shape
    bases = voxel_weights.shape[1]
    half = planes // 2
    assert half == RADIUS and planes % 2 == 0
    quarters = lax.axis_size("view")
    depths = lax.axis_size("depth")
    span = height // quarters
    views_total = views * quarters
    voxel_total = planes * depths * height * breadth
    parity = lax.rem(lax.axis_index("depth"), 2).astype(jnp.int32)
    first_view, first_plane = lax.axis_index("view") * views, lax.axis_index("depth") * planes
    halves = [
        jnp.stack([at, first_view, first_plane + at * half]).astype(jnp.int32) for at in (parity, 1 - parity)
    ]

    def swap(values, which):
        pairs = []
        for i in range(1 - which, depths - 1, 2):
            pairs += [(i, i + 1), (i + 1, i)]
        return lax.ppermute(values, "depth", pairs)

    def shape(*dims, dtype=F32):
        return jax.ShapeDtypeStruct(dims, dtype)

    x_shape = shape(views, bases, breadth, breadth, dtype=BF16)
    y_shape = shape(views, bases * height, height, dtype=BF16)
    gain_shape = shape(views, bases, breadth)
    yt_shape = shape(views, height, bases * height, dtype=BF16)
    noise_shape = shape(noise_rows(bases, height), breadth)
    group_shape = shape(quarters, half, span, breadth)
    field_shape = shape(views, half, height, breadth)
    fidelity_shape = shape(views, 8, breadth)
    current_shape = shape(half, span, breadth)
    volume = views * bases * half * height * breadth

    x_mat, xt_mat, y_mat, yt_mat, axial, noise, gain = call(
        prepare_kernel, (views,), [SMEM, per_view(lateral_taps.shape), whole(axial_taps.shape)],
        (x_shape, x_shape, y_shape, yt_shape, shape(*axial_taps.shape), noise_shape, gain_shape),
        (per_view(x_shape.shape), per_view(x_shape.shape), per_view(y_shape.shape), per_view(yt_shape.shape),
         whole(axial_taps.shape), whole(noise_shape.shape), per_view(gain_shape.shape)),
        prefetch=0, cost=(volume, volume),
    )(lateral_taps, lateral_taps, axial_taps)

    weights_buf = pltpu.VMEM((views, bases, half, height, breadth), BF16)
    x_buf = pltpu.VMEM(x_shape.shape, BF16)
    yt_buf = pltpu.VMEM(yt_shape.shape, BF16)
    sems = pltpu.SemaphoreType.DMA((views, 5))
    mixed_buf = pltpu.VMEM((half, 2 * bases * height, breadth), BF16)

    def ones_half(which, after):
        return call(
            ones_kernel, (views,), [ANY] * 4, field_shape, per_view(field_shape.shape),
            [weights_buf, x_buf, yt_buf, sems, mixed_buf], vmem=20, cost=(2 * volume * (breadth + height), 4 * volume),
        )(halves[which], voxel_weights, xt_mat, yt_mat, after)

    def step_half(which, halo, near, far, after, last):
        out = call(
            step_kernel if last else plain_step_kernel, (views,),
            [SMEM] + [whole(group_shape.shape)] * 3 + [whole(noise_shape.shape), per_view(gain_shape.shape), per_view(y_shape.shape)] + [ANY] * 6,
            (field_shape, fidelity_shape) if last else field_shape,
            (per_view(field_shape.shape), per_view(fidelity_shape.shape)) if last else per_view(field_shape.shape),
            [weights_buf, pltpu.VMEM((views, half, height, breadth), F32), x_buf, x_buf, yt_buf, sems,
             pltpu.VMEM((half, 2 * height, breadth), BF16),
             pltpu.VMEM((bases, half * height, breadth), BF16), mixed_buf],
            vmem=36, cost=(4 * volume * (breadth + height), 4 * volume),
        )(halves[which], axial, halo, near, far, noise, gain, y_mat, observed, voxel_weights, x_mat, xt_mat, yt_mat, after)
        return out if last else (out, None)

    def depth_half(which, halo, near, far, after, scale=None):
        scales_in = () if scale is None else (scale,)
        return call(
            scale_kernel if scale is None else log_kernel, (1,),
            [SMEM] + [whole(field_shape.shape)] * 3 + [whole(group_shape.shape)] * len(scales_in) + [ANY],
            group_shape, whole(group_shape.shape), cost=(20 * near.size, 16 * near.size),
        )(halves[which], axial, halo, near, far, *scales_in, after)

    own_block = pl.BlockSpec((1, half, span, breadth), lambda _, place: (place[0], 0, 0, 0))
    own_cost = half * span * breadth

    def share(which):
        own = estimate.reshape(2, half, span, breadth)
        return call(
            share_kernel, (1,), [own_block], (group_shape, current_shape),
            (whole(group_shape.shape), whole(current_shape.shape)), cost=(own_cost, 8 * own_cost),
        )(halves[which], own)

    def update(pieces, current):
        def kernel(pieces_ref, current_ref, copies_ref, new_ref):
            new_ref[...] = corrected(pieces_ref, current_ref, views_total)
            for q in range(quarters):
                copies_ref[q] = new_ref[...]

        return call(
            kernel, (1,), [whole(group_shape.shape), whole(current_shape.shape)], (group_shape, current_shape),
            (whole(group_shape.shape), whole(current_shape.shape)), prefetch=0, cost=(8 * own_cost, 40 * own_cost),
        )(pieces, current)

    def finish(which, pieces, current, so_far):
        aliased = so_far is not None

        def kernel(place_ref, pieces_ref, current_ref, *rest):
            rest[-1][0] = corrected(pieces_ref, current_ref, views_total)

        return call(
            kernel, (1,), [whole(group_shape.shape), whole(current_shape.shape)] + [ANY] * aliased,
            shape(2, half, span, breadth), own_block,
            cost=(8 * own_cost, 24 * own_cost), input_output_aliases={3: 0} if aliased else {},
        )(halves[which], pieces, current, *((so_far,) if aliased else ()))

    def exchange(values):
        return lax.all_to_all(values, "view", 0, 0)

    copies, current = zip(*[share(k) for k in range(2)])
    groups = [exchange(copies[k]) for k in range(2)]
    sens, sens_halo = [None, None], [None, None]
    for k in range(2):
        sens[k] = ones_half(k, sens[0] if k else axial)
        sens_halo[k] = swap(sens[k], k)
    scales = [None, None]
    for iteration in range(ITERS):
        last = iteration == ITERS - 1
        halo = [swap(groups[k], k) for k in range(2)]
        fields, parts, fields_halo = [None, None], [None, None], [None, None]
        for k in range(2):
            fields[k], parts[k] = step_half(k, halo[k], groups[k], groups[1 - k], fields[0] if k else axial, last)
            fields_halo[k] = swap(fields[k], k)
        if iteration == 0:
            for k in range(2):
                scales[k] = depth_half(k, sens_halo[k], sens[k], sens[1 - k], scales[0] if k else axial)
        order = (1, 0) if last else (0, 1)
        pieces, logs = [None, None], axial
        for k in order:
            logs = depth_half(k, fields_halo[k], fields[k], fields[1 - k], logs, scales[k])
            pieces[k] = exchange(logs)
        if not last:
            copies, current = zip(*[update(pieces[k], current[k]) for k in range(2)])
            groups = [exchange(copies[k]) for k in range(2)]
    local = jnp.sum(parts[0] + parts[1], axis=(1, 2))
    updated = finish(order[0], pieces[order[0]], current[order[0]], None)
    local, updated = lax.optimization_barrier((local, updated))
    divergence = lax.psum(local, "depth") / voxel_total
    updated = finish(order[1], pieces[order[1]], current[order[1]], updated)
    return updated.reshape(estimate.shape), divergence


def solution(mesh):
    placed = (
        P("depth", "view", None),
        P("view", "depth", None, None),
        P("view", None, "depth", None, None),
        P("view", None, None, None),
        P("view", None),
    )
    return jax.shard_map(
        body,
        mesh=mesh,
        in_specs=placed,
        out_specs=(P("depth", "view", None), P("view")),
        check_vma=False,
    )
```

profile of v0, /device:TPU:0, one launch (start us, length us, event | category | flops | bytes accessed | tf_op | source)
XLA Modules:
  0.0 198.1 jit_solution(13924458716570702094)
XLA Ops:
  3.1 5.2 %all-to-all-start = ((f32[4,4,32,256]{3,2,1,0:T(8,128)}), f32[4,4,32,256]{3,2,1,0:T(8,128)}, u32[]{:S(2)}, u32[]{:S(2)}) async-start(f32[4,4,32,256]{3,2,1,0:T(8,128)} %get-tuple-element.24), calls=%async_computation | async-start | bytes 1048576 | tf_op jit(solution)/shard_map/all_to_all | solution.py:385
  11.3 5.5 %all-to-all-done.refs_3_.refs_4_ = f32[4,4,32,256]{3,2,1,0:T(8,128)} async-done(((f32[4,4,32,256]{3,2,1,0:T(8,128)}), f32[4,4,32,256]{3,2,1,0:T(8,128)}, u32[]{:S(2)}, u32[]{:S(2)}) %all-to-all-start) | async-done | bytes 524320 | tf_op jit(solution)/shard_map/all_to_all | solution.py:385
  16.8 4.1 %all-to-all-start.1 = ((f32[4,4,32,256]{3,2,1,0:T(8,128)}), f32[4,4,32,256]{3,2,1,0:T(8,128)}, u32[]{:S(2)}, u32[]{:S(2)}) async-start(f32[4,4,32,256]{3,2,1,0:T(8,128)} %get-tuple-element.25), calls=%async_computation.1 | async-start | bytes 1048576 | tf_op jit(solution)/shard_map/all_to_all | solution.py:385
  22.4 6.8 %shard_map.68 = (bf16[2,8,256,256]{3,2,1,0:T(8,128)(2,1)S(1)}, bf16[2,8,256,256]{3,2,1,0:T(8,128)(2,1)S(1)}, bf16[2,1024,128]{2,1,0:T(8,128)(2,1)S(1)}, bf16[2,1...) custom-call(f32[2,8,2,9]{3,2,1,0:T(2,128)S(1)} %copy-done.28, ...), custom_call_target="tpu_custom_call" | custom-call | flops 2097152 | bytes 2097152 | tf_op jit(solution)/shard_map/pallas_call | solution.py:310
  31.8 2.4 %collective-permute-start.2 = (f32[4,4,32,256]{3,2,1,0:T(8,128)}, f32[4,4,32,256]{3,2,1,0:T(8,128)S(1)}, u32[]{:S(2)}, u32[]{:S(2)}) collective-permute-start(f32[4,4,32,256]{3,2,1,0:T(8,128)} %all-to-all-done.1.refs_4_.refs_3_), channel_id=1, source_target_pairs={{0,1},{1,0},{2,3},{3,2},{4,5},{5,4},{6,7},{7,6},{8,9},{9,8},{10,11... | collective-permute-start | bytes 1572872 | tf_op jit(solution)/shard_map/ppermute | solution.py:294
  34.2 3.4 %copy-done = bf16[2,8,8,128,256]{4,3,2,1,0:T(8,128)(2,1)S(1)} copy-done((bf16[2,8,8,128,256]{4,3,2,1,0:T(8,128)(2,1)S(1)}, bf16[2,8,8,128,256]{4,3,2,1,0:T(8,128)(2,1)}, u32[]{:S(2)}) %copy-start) | copy-done | bytes 8388632
  37.6 3.6 %shard_map.73.after_any.near_ref.far_ref = f32[2,4,128,256]{3,2,1,0:T(8,128)S(1)} custom-call(s32[3]{0:T(128)S(1)} %pad_add_fusion.place_ref.refs_0_, bf16[2,8,8,128,256]{4,3,2,1,0:T(8,128)(2,1)S(1)} %copy-done, bf16[2,8,256,256]{3,2,1,0:T(8,128)(2,1)S(1)} %get-tuple-element.30.refs_11_.xt_any, bf16[2,128,1024]{2,1,0:T(8,128)(2,1)S(1)} %get-tuple-element.31.refs_12_.yt_any, ...), custom_call_target="tpu_custom_call" | custom-call | flops 1610612736 | bytes 8388608 | tf_op jit(solution)/shard_map/pallas_call | solution.py:325
  42.0 9.7 %shard_map.71.refs_13_.near_ref.far_ref = f32[2,4,128,256]{3,2,1,0:T(8,128)S(1)} custom-call(s32[3]{0:T(128)S(1)} %pad_add_fusion.place_ref.refs_0_, f32[2,9]{1,0:T(2,128)S(1)} %get-tuple-element.23.refs_1_.refs_13_.after_any.axial_ref, f32[4,4,32,256]{3,2,1,0:T(8,128)} %collective-permute-done.refs_2_, f32[4,4,32,256]{3,2,1,0:T(8,128)} %all-to-all-done.refs_3_.refs_4_, ...), custom_call_target="tpu_custom_call" | custom-call | flops 3221225472 | bytes 8388608 | tf_op jit(solution)/shard_map/pallas_call | solution.py:331
  52.7 4.5 %shard_map.74.far_ref.near_ref = f32[2,4,128,256]{3,2,1,0:T(8,128)} custom-call(s32[3]{0:T(128)S(1)} %pad_add_fusion.1.place_ref.refs_0_, bf16[2,8,8,128,256]{4,3,2,1,0:T(8,128)(2,1)S(1)} %bitcast.8, bf16[2,8,256,256]{3,2,1,0:T(8,128)(2,1)S(1)} %get-tuple-element.30.refs_11_.xt_any, bf16[2,128,1024]{2,1,0:T(8,128)(2,1)S(1)} %get-tuple-element.31.refs_12_.yt_any, ...), custom_call_target="tpu_custom_call" | custom-call | flops 1610612736 | bytes 8388608 | tf_op jit(solution)/shard_map/pallas_call | solution.py:325
  57.2 4.4 %collective-permute-start.6 = (f32[2,4,128,256]{3,2,1,0:T(8,128)}, f32[2,4,128,256]{3,2,1,0:T(8,128)}, u32[]{:S(2)}, u32[]{:S(2)}) collective-permute-start(f32[2,4,128,256]{3,2,1,0:T(8,128)} %shard_map.74.far_ref.near_ref), channel_id=1, source_target_pairs={{0,1},{1,0},{2,3},{3,2},{4,5},{5,4},{6,7},{7,6},{8,9},{9,8},{10,11... | collective-permute-start | bytes 3145736 | tf_op jit(solution)/shard_map/ppermute | solution.py:294
  61.6 10.1 %shard_map.72.far_ref.near_ref = f32[2,4,128,256]{3,2,1,0:T(8,128)} custom-call(s32[3]{0:T(128)S(1)} %pad_add_fusion.1.place_ref.refs_0_, f32[2,9]{1,0:T(2,128)S(1)} %get-tuple-element.23.refs_1_.refs_13_.after_any.axial_ref, f32[4,4,32,256]{3,2,1,0:T(8,128)S(1)} %collective-permute-done.2.refs_2_, f32[4,4,32,256]{3,2,1,0:T(8,128)} %all-to-all-done.1.refs_4_.refs_3_, ...), custom_call_target="tpu_custom_call" | custom-call | flops 3221225472 | bytes 8388608 | tf_op jit(solution)/shard_map/pallas_call | solution.py:331
  71.8 2.5 %shard_map.75.scale_ref.after_any = f32[4,4,32,256]{3,2,1,0:T(8,128)S(1)} custom-call(s32[3]{0:T(128)S(1)} %pad_add_fusion.place_ref.refs_0_, f32[2,9]{1,0:T(2,128)S(1)} %get-tuple-element.23.refs_1_.refs_13_.after_any.axial_ref, f32[2,4,128,256]{3,2,1,0:T(8,128)S(1)} %collective-permute-done.3.halo_ref, ...), custom_call_target="tpu_custom_call" | custom-call | flops 5242880 | bytes 4194304 | tf_op jit(solution)/shard_map/pallas_call | solution.py:345
  74.4 2.5 %shard_map.76.after_any = f32[4,4,32,256]{3,2,1,0:T(8,128)S(1)} custom-call(s32[3]{0:T(128)S(1)} %pad_add_fusion.place_ref.refs_0_, f32[2,9]{1,0:T(2,128)S(1)} %get-tuple-element.23.refs_1_.refs_13_.after_any.axial_ref, f32[2,4,128,256]{3,2,1,0:T(8,128)S(1)} %collective-permute-done.1.halo_ref, f32[2,4,128,256]{3,2,1,0:T(8,128)S(1)} %shard_map.71.refs_13_.near_ref.far_ref, ...), custom_call_target="tpu_custom_call" | custom-call | flops 5242880 | bytes 4194304 | tf_op jit(solution)/shard_map/pallas_call | solution.py:345
  77.7 4.1 %all-to-all-start.2 = ((f32[4,4,32,256]{3,2,1,0:T(8,128)}), f32[4,4,32,256]{3,2,1,0:T(8,128)}, u32[]{:S(2)}, u32[]{:S(2)}) async-start(f32[4,4,32,256]{3,2,1,0:T(8,128)} %copy-done.17), calls=%async_computation.2 | async-start | bytes 1048576 | tf_op jit(solution)/shard_map/all_to_all | solution.py:385
  83.1 2.8 %shard_map.78.scale_ref = f32[4,4,32,256]{3,2,1,0:T(8,128)S(1)} custom-call(s32[3]{0:T(128)S(1)} %pad_add_fusion.1.place_ref.refs_0_, f32[2,9]{1,0:T(2,128)S(1)} %get-tuple-element.23.refs_1_.refs_13_.after_any.axial_ref, f32[2,4,128,256]{3,2,1,0:T(8,128)} %collective-permute-done.6.halo_ref, f32[2,4,128,256]{3,2,1,0:T(8,128)} %shard_map.74.far_ref.near_ref, ...), custom_call_target="tpu_custom_call" | custom-call | flops 5242880 | bytes 4194304 | tf_op jit(solution)/shard_map/pallas_call | solution.py:345
  85.9 2.8 %shard_map.79 = f32[4,4,32,256]{3,2,1,0:T(8,128)S(1)} custom-call(s32[3]{0:T(128)S(1)} %pad_add_fusion.1.place_ref.refs_0_, f32[2,9]{1,0:T(2,128)S(1)} %get-tuple-element.23.refs_1_.refs_13_.after_any.axial_ref, f32[2,4,128,256]{3,2,1,0:T(8,128)} %collective-permute-done.5.halo_ref, f32[2,4,128,256]{3,2,1,0:T(8,128)} %shard_map.72.far_ref.near_ref, ...), custom_call_target="tpu_custom_call" | custom-call | flops 5242880 | bytes 4194304 | tf_op jit(solution)/shard_map/pallas_call | solution.py:345
  91.1 4.1 %all-to-all-start.4 = ((f32[4,4,32,256]{3,2,1,0:T(8,128)}), f32[4,4,32,256]{3,2,1,0:T(8,128)}, u32[]{:S(2)}, u32[]{:S(2)}) async-start(f32[4,4,32,256]{3,2,1,0:T(8,128)} %copy-done.21), calls=%async_computation.4 | async-start | bytes 1048576 | tf_op jit(solution)/shard_map/all_to_all | solution.py:385
  97.1 6.6 %all-to-all-done.4.pieces_ref = f32[4,4,32,256]{3,2,1,0:T(8,128)} async-done(((f32[4,4,32,256]{3,2,1,0:T(8,128)}), f32[4,4,32,256]{3,2,1,0:T(8,128)}, u32[]{:S(2)}, u32[]{:S(2)}) %all-to-all-start.4) | async-done | bytes 524320 | tf_op jit(solution)/shard_map/all_to_all | solution.py:385
  103.8 4.2 %all-to-all-start.3 = ((f32[4,4,32,256]{3,2,1,0:T(8,128)}), f32[4,4,32,256]{3,2,1,0:T(8,128)}, u32[]{:S(2)}, u32[]{:S(2)}) async-start(f32[4,4,32,256]{3,2,1,0:T(8,128)} %copy-done.24), calls=%async_computation.3 | async-start | bytes 1048576 | tf_op jit(solution)/shard_map/all_to_all | solution.py:385
  110.8 4.9 %all-to-all-done.3.near_ref.far_ref = f32[4,4,32,256]{3,2,1,0:T(8,128)} async-done(((f32[4,4,32,256]{3,2,1,0:T(8,128)}), f32[4,4,32,256]{3,2,1,0:T(8,128)}, u32[]{:S(2)}, u32[]{:S(2)}) %all-to-all-start.3) | async-done | bytes 524320 | tf_op jit(solution)/shard_map/all_to_all | solution.py:385
  115.6 4.1 %all-to-all-start.5 = ((f32[4,4,32,256]{3,2,1,0:T(8,128)}), f32[4,4,32,256]{3,2,1,0:T(8,128)}, u32[]{:S(2)}, u32[]{:S(2)}) async-start(f32[4,4,32,256]{3,2,1,0:T(8,128)} %copy-done.25), calls=%async_computation.5 | async-start | bytes 1048576 | tf_op jit(solution)/shard_map/all_to_all | solution.py:385
  121.3 5.4 %all-to-all-done.5.far_ref.near_ref = f32[4,4,32,256]{3,2,1,0:T(8,128)} async-done(((f32[4,4,32,256]{3,2,1,0:T(8,128)}), f32[4,4,32,256]{3,2,1,0:T(8,128)}, u32[]{:S(2)}, u32[]{:S(2)}) %all-to-all-start.5) | async-done | bytes 524320 | tf_op jit(solution)/shard_map/all_to_all | solution.py:385
  128.3 1.6 copy-done.5
  132.3 10.5 %shard_map.81 = (f32[2,4,128,256]{3,2,1,0:T(8,128)}, f32[2,8,256]{2,1,0:T(8,128)S(1)}) custom-call(s32[3]{0:T(128)S(1)} %pad_add_fusion.place_ref.refs_0_, f32[2,9]{1,0:T(2,128)S(1)} %get-tuple-element.23.refs_1_.refs_13_.after_any.axial_ref, f32[4,4,32,256]{3,2,1,0:T(8,128)} %collective-permute-done.4.halo_ref, ...), custom_call_target="tpu_custom_call" | custom-call | flops 3221225472 | bytes 8388608 | tf_op jit(solution)/shard_map/pallas_call | solution.py:331
  142.8 9.5 %shard_map.82 = (f32[2,4,128,256]{3,2,1,0:T(8,128)S(1)}, f32[2,8,256]{2,1,0:T(8,128)S(1)}) custom-call(s32[3]{0:T(128)S(1)} %pad_add_fusion.1.place_ref.refs_0_, f32[2,9]{1,0:T(2,128)S(1)} %get-tuple-element.23.refs_1_.refs_13_.after_any.axial_ref, f32[4,4,32,256]{3,2,1,0:T(8,128)S(1)} %collective-permute-done.8.halo_ref, ...), custom_call_target="tpu_custom_call" | custom-call | flops 3221225472 | bytes 8388608 | tf_op jit(solution)/shard_map/pallas_call | solution.py:331
  152.3 4.0 %collective-permute-start.9 = (f32[2,4,128,256]{3,2,1,0:T(8,128)S(1)}, f32[2,4,128,256]{3,2,1,0:T(8,128)S(1)}, u32[]{:S(2)}, u32[]{:S(2)}) collective-permute-start(f32[2,4,128,256]{3,2,1,0:T(8,128)S(1)} %get-tuple-element.37.near_ref.far_ref), channel_id=1, source_target_pairs={{0,1},{1,0},{2,3},{3,2},{4,5},{5,4},{6,7},{7,6},{8,9},{9,8},{10,11... | collective-permute-start | bytes 3145736 | tf_op jit(solution)/shard_map/ppermute | solution.py:294
  158.6 3.3 %shard_map.83.after_any = f32[4,4,32,256]{3,2,1,0:T(8,128)} custom-call(s32[3]{0:T(128)S(1)} %pad_add_fusion.1.place_ref.refs_0_, f32[2,9]{1,0:T(2,128)S(1)} %get-tuple-element.23.refs_1_.refs_13_.after_any.axial_ref, f32[2,4,128,256]{3,2,1,0:T(8,128)S(1)} %collective-permute-done.9.halo_ref, f32[2,4,128,256]{3,2,1,0:T(8,128)S(1)} %get-tuple-element.37.near_ref.far_ref, ...), custom_call_target="tpu_custom_call" | custom-call | flops 5242880 | bytes 4194304 | tf_op jit(solution)/shard_map/pallas_call | solution.py:345
  162.9 4.1 %all-to-all-start.7 = ((f32[4,4,32,256]{3,2,1,0:T(8,128)}), f32[4,4,32,256]{3,2,1,0:T(8,128)S(1)}, u32[]{:S(2)}, u32[]{:S(2)}) async-start(f32[4,4,32,256]{3,2,1,0:T(8,128)} %shard_map.83.after_any), calls=%async_computation.7 | async-start | bytes 1048576 | tf_op jit(solution)/shard_map/all_to_all | solution.py:385
  168.3 3.3 %shard_map.84 = f32[4,4,32,256]{3,2,1,0:T(8,128)} custom-call(s32[3]{0:T(128)S(1)} %pad_add_fusion.place_ref.refs_0_, f32[2,9]{1,0:T(2,128)S(1)} %get-tuple-element.23.refs_1_.refs_13_.after_any.axial_ref, f32[2,4,128,256]{3,2,1,0:T(8,128)S(1)} %collective-permute-done.7.halo_ref, f32[2,4,128,256]{3,2,1,0:T(8,128)} %get-tuple-element.36.after_any.far_ref.near_ref, ...), custom_call_target="tpu_custom_call" | custom-call | flops 5242880 | bytes 4194304 | tf_op jit(solution)/shard_map/pallas_call | solution.py:345
  171.6 4.6 %all-to-all-done.7.pieces_ref = f32[4,4,32,256]{3,2,1,0:T(8,128)S(1)} async-done(((f32[4,4,32,256]{3,2,1,0:T(8,128)}), f32[4,4,32,256]{3,2,1,0:T(8,128)S(1)}, u32[]{:S(2)}, u32[]{:S(2)}) %all-to-all-start.7) | async-done | bytes 524320 | tf_op jit(solution)/shard_map/all_to_all | solution.py:385
  176.2 3.5 %all-to-all-start.6 = ((f32[4,4,32,256]{3,2,1,0:T(8,128)}), f32[4,4,32,256]{3,2,1,0:T(8,128)S(1)}, u32[]{:S(2)}, u32[]{:S(2)}) async-start(f32[4,4,32,256]{3,2,1,0:T(8,128)} %shard_map.84), calls=%async_computation.6 | async-start | bytes 1048576 | tf_op jit(solution)/shard_map/all_to_all | solution.py:385
  181.1 15.3 %psum.7 = f32[2]{0:T(128)S(1)} all-reduce(f32[2]{0:T(128)S(1)} %add_reduce_fusion), channel_id=1, replica_groups=mesh['view'=4,'depth'=8] {'depth'}, use_global_device_ids=true, to_apply=%region_1.0 | all-reduce | flops 2 | bytes 16 | tf_op jit(solution)/shard_map/psum | solution.py:415
  (93 shorter events, 33.4 us)
Async XLA Ops:
  0.6 21.8 %copy-start.28 = (f32[2,8,2,9]{3,2,1,0:T(2,128)S(1)}, f32[2,8,2,9]{3,2,1,0:T(2,128)}, u32[]{:S(2)}) copy-start(f32[2,8,2,9]{3,2,1,0:T(2,128)} %lateral_ref.1) | copy-start | bytes 3460
  0.6 21.8 %copy-start.29 = (f32[2,9]{1,0:T(2,128)S(1)}, f32[2,9]{1,0:T(2,128)}, u32[]{:S(2)}) copy-start(f32[2,9]{1,0:T(2,128)} %axial_ref.1) | copy-start | bytes 220
  3.1 13.7 %all-to-all-start = ((f32[4,4,32,256]{3,2,1,0:T(8,128)}), f32[4,4,32,256]{3,2,1,0:T(8,128)}, u32[]{:S(2)}, u32[]{:S(2)}) async-start(f32[4,4,32,256]{3,2,1,0:T(8,128)} %get-tuple-element.24), calls=%async_computation | async-start | bytes 1048576 | tf_op jit(solution)/shard_map/all_to_all | solution.py:385
  16.8 15.0 %all-to-all-start.1 = ((f32[4,4,32,256]{3,2,1,0:T(8,128)}), f32[4,4,32,256]{3,2,1,0:T(8,128)}, u32[]{:S(2)}, u32[]{:S(2)}) async-start(f32[4,4,32,256]{3,2,1,0:T(8,128)} %get-tuple-element.25), calls=%async_computation.1 | async-start | bytes 1048576 | tf_op jit(solution)/shard_map/all_to_all | solution.py:385
  20.9 21.0 %collective-permute-start = (f32[4,4,32,256]{3,2,1,0:T(8,128)}, f32[4,4,32,256]{3,2,1,0:T(8,128)}, u32[]{:S(2)}, u32[]{:S(2)}) collective-permute-start(f32[4,4,32,256]{3,2,1,0:T(8,128)} %all-to-all-done.refs_3_.refs_4_), channel_id=1, source_target_pairs={{1,2},{2,1},{3,4},{4,3},{5,6},{6,5},{9,10},{10,9},{11,12},{12,11},... | collective-permute-start | bytes 1572872 | tf_op jit(solution)/shard_map/ppermute | solution.py:294
  31.8 29.8 %copy-start.13 = (bf16[2,1024,128]{2,1,0:T(8,128)(2,1)}, bf16[2,1024,128]{2,1,0:T(8,128)(2,1)S(1)}, u32[]{:S(2)}) copy-start(bf16[2,1024,128]{2,1,0:T(8,128)(2,1)S(1)} %get-tuple-element.28.refs_7_.y_ref) | copy-start | bytes 1572868
  31.8 29.8 %collective-permute-start.2 = (f32[4,4,32,256]{3,2,1,0:T(8,128)}, f32[4,4,32,256]{3,2,1,0:T(8,128)S(1)}, u32[]{:S(2)}, u32[]{:S(2)}) collective-permute-start(f32[4,4,32,256]{3,2,1,0:T(8,128)} %all-to-all-done.1.refs_4_.refs_3_), channel_id=1, source_target_pairs={{0,1},{1,0},{2,3},{3,2},{4,5},{5,4},{6,7},{7,6},{8,9},{9,8},{10,11... | collective-permute-start | bytes 1572872 | tf_op jit(solution)/shard_map/ppermute | solution.py:294
  34.2 3.4 %copy-start = (bf16[2,8,8,128,256]{4,3,2,1,0:T(8,128)(2,1)S(1)}, bf16[2,8,8,128,256]{4,3,2,1,0:T(8,128)(2,1)}, u32[]{:S(2)}) copy-start(bf16[2,8,8,128,256]{4,3,2,1,0:T(8,128)(2,1)} %weights_any.7) | copy-start | bytes 25165828
  37.6 4.4 %copy-start.1 = (f32[2,8,128,256]{3,2,1,0:T(8,128)S(1)}, f32[2,8,128,256]{3,2,1,0:T(8,128)}, u32[]{:S(2)}) copy-start(f32[2,8,128,256]{3,2,1,0:T(8,128)} %counts_any.3) | copy-start | bytes 6291460
  37.6 4.4 %copy-start.4 = (bf16[2,8,256,256]{3,2,1,0:T(8,128)(2,1)S(1)}, bf16[2,8,256,256]{3,2,1,0:T(8,128)(2,1)}, u32[]{:S(2)}) copy-start(bf16[2,8,256,256]{3,2,1,0:T(8,128)(2,1)} %copy-done.3) | copy-start | bytes 6291460
  37.6 4.4 %copy-start.7 = (f32[1536,256]{1,0:T(8,128)S(1)}, f32[1536,256]{1,0:T(8,128)}, u32[]{:S(2)}) copy-start(f32[1536,256]{1,0:T(8,128)} %copy-done.6) | copy-start | bytes 4718596
  37.6 15.1 %slice-start = ((s8[8388608]{0:T(1024)(128)(4,1)}), s8[4194304]{0:T(1024)(128)(4,1)S(1)}, s32[]{:S(2)}) async-start(s8[8388608]{0:T(1024)(128)(4,1)} %bitcast.7), calls=%async_computation.8 | async-start | bytes 8388608
  41.2 30.6 %copy-start.9 = (f32[2,4,128,256]{3,2,1,0:T(8,128)}, f32[2,4,128,256]{3,2,1,0:T(8,128)S(1)}, u32[]{:S(2)}) copy-start(f32[2,4,128,256]{3,2,1,0:T(8,128)S(1)} %shard_map.73.after_any.near_ref.far_ref) | copy-start | bytes 3145732
  41.2 30.6 %collective-permute-start.3 = (f32[2,4,128,256]{3,2,1,0:T(8,128)S(1)}, f32[2,4,128,256]{3,2,1,0:T(8,128)S(1)}, u32[]{:S(2)}, u32[]{:S(2)}) collective-permute-start(f32[2,4,128,256]{3,2,1,0:T(8,128)S(1)} %shard_map.73.after_any.near_ref.far_ref), channel_id=1, source_target_pairs={{1,2},{2,1},{3,4},{4,3},{5,6},{6,5},{9,10},{10,9},{11,12},{12,11},... | collective-permute-start | bytes 3145736 | tf_op jit(solution)/shard_map/ppermute | solution.py:294
  42.0 10.7 %slice-start.1 = ((s8[8388608]{0:T(1024)(128)(4,1)}), s8[4194304]{0:T(1024)(128)(4,1)S(1)}, s32[]{:S(2)}) async-start(s8[8388608]{0:T(1024)(128)(4,1)} %bitcast.7), calls=%async_computation.9 | async-start | bytes 8388608
  51.8 22.6 %copy-start.11 = (f32[2,4,128,256]{3,2,1,0:T(8,128)}, f32[2,4,128,256]{3,2,1,0:T(8,128)S(1)}, u32[]{:S(2)}) copy-start(f32[2,4,128,256]{3,2,1,0:T(8,128)S(1)} %shard_map.71.refs_13_.near_ref.far_ref) | copy-start | bytes 3145732
  51.8 22.6 %collective-permute-start.1 = (f32[2,4,128,256]{3,2,1,0:T(8,128)S(1)}, f32[2,4,128,256]{3,2,1,0:T(8,128)S(1)}, u32[]{:S(2)}, u32[]{:S(2)}) collective-permute-start(f32[2,4,128,256]{3,2,1,0:T(8,128)S(1)} %shard_map.71.refs_13_.near_ref.far_ref), channel_id=1, source_target_pairs={{1,2},{2,1},{3,4},{4,3},{5,6},{6,5},{9,10},{10,9},{11,12},{12,11},... | collective-permute-start | bytes 3145736 | tf_op jit(solution)/shard_map/ppermute | solution.py:294
  57.2 24.6 %collective-permute-start.6 = (f32[2,4,128,256]{3,2,1,0:T(8,128)}, f32[2,4,128,256]{3,2,1,0:T(8,128)}, u32[]{:S(2)}, u32[]{:S(2)}) collective-permute-start(f32[2,4,128,256]{3,2,1,0:T(8,128)} %shard_map.74.far_ref.near_ref), channel_id=1, source_target_pairs={{0,1},{1,0},{2,3},{3,2},{4,5},{5,4},{6,7},{7,6},{8,9},{9,8},{10,11... | collective-permute-start | bytes 3145736 | tf_op jit(solution)/shard_map/ppermute | solution.py:294
  71.7 14.2 %collective-permute-start.5 = (f32[2,4,128,256]{3,2,1,0:T(8,128)}, f32[2,4,128,256]{3,2,1,0:T(8,128)}, u32[]{:S(2)}, u32[]{:S(2)}) collective-permute-start(f32[2,4,128,256]{3,2,1,0:T(8,128)} %shard_map.72.far_ref.near_ref), channel_id=1, source_target_pairs={{0,1},{1,0},{2,3},{3,2},{4,5},{5,4},{6,7},{7,6},{8,9},{9,8},{10,11... | collective-permute-start | bytes 3145736 | tf_op jit(solution)/shard_map/ppermute | solution.py:294
  77.7 13.4 %all-to-all-start.2 = ((f32[4,4,32,256]{3,2,1,0:T(8,128)}), f32[4,4,32,256]{3,2,1,0:T(8,128)}, u32[]{:S(2)}, u32[]{:S(2)}) async-start(f32[4,4,32,256]{3,2,1,0:T(8,128)} %copy-done.17), calls=%async_computation.2 | async-start | bytes 1048576 | tf_op jit(solution)/shard_map/all_to_all | solution.py:385
  83.1 2.8 %copy-start.12 = (f32[2,4,128,256]{3,2,1,0:T(8,128)S(1)}, f32[2,4,128,256]{3,2,1,0:T(8,128)}, u32[]{:S(2)}) copy-start(f32[2,4,128,256]{3,2,1,0:T(8,128)} %copy-done.11) | copy-start | bytes 3145732
  83.1 2.8 %copy-start.18 = (f32[4,4,32,256]{3,2,1,0:T(8,128)S(1)}, f32[4,4,32,256]{3,2,1,0:T(8,128)}, u32[]{:S(2)}) copy-start(f32[4,4,32,256]{3,2,1,0:T(8,128)} %copy-done.17) | copy-start | bytes 1572868
  91.1 12.7 %all-to-all-start.4 = ((f32[4,4,32,256]{3,2,1,0:T(8,128)}), f32[4,4,32,256]{3,2,1,0:T(8,128)}, u32[]{:S(2)}, u32[]{:S(2)}) async-start(f32[4,4,32,256]{3,2,1,0:T(8,128)} %copy-done.21), calls=%async_computation.4 | async-start | bytes 1048576 | tf_op jit(solution)/shard_map/all_to_all | solution.py:385
  103.8 11.9 %all-to-all-start.3 = ((f32[4,4,32,256]{3,2,1,0:T(8,128)}), f32[4,4,32,256]{3,2,1,0:T(8,128)}, u32[]{:S(2)}, u32[]{:S(2)}) async-start(f32[4,4,32,256]{3,2,1,0:T(8,128)} %copy-done.24), calls=%async_computation.3 | async-start | bytes 1048576 | tf_op jit(solution)/shard_map/all_to_all | solution.py:385
  115.6 11.0 %all-to-all-start.5 = ((f32[4,4,32,256]{3,2,1,0:T(8,128)}), f32[4,4,32,256]{3,2,1,0:T(8,128)}, u32[]{:S(2)}, u32[]{:S(2)}) async-start(f32[4,4,32,256]{3,2,1,0:T(8,128)} %copy-done.25), calls=%async_computation.5 | async-start | bytes 1048576 | tf_op jit(solution)/shard_map/all_to_all | solution.py:385
  119.8 6.9 %collective-permute-start.4 = (f32[4,4,32,256]{3,2,1,0:T(8,128)}, f32[4,4,32,256]{3,2,1,0:T(8,128)}, u32[]{:S(2)}, u32[]{:S(2)}) collective-permute-start(f32[4,4,32,256]{3,2,1,0:T(8,128)} %all-to-all-done.3.near_ref.far_ref), channel_id=1, source_target_pairs={{1,2},{2,1},{3,4},{4,3},{5,6},{6,5},{9,10},{10,9},{11,12},{12,11},... | collective-permute-start | bytes 1572872 | tf_op jit(solution)/shard_map/ppermute | solution.py:294
  126.7 16.1 %collective-permute-start.8 = (f32[4,4,32,256]{3,2,1,0:T(8,128)}, f32[4,4,32,256]{3,2,1,0:T(8,128)S(1)}, u32[]{:S(2)}, u32[]{:S(2)}) collective-permute-start(f32[4,4,32,256]{3,2,1,0:T(8,128)} %all-to-all-done.5.far_ref.near_ref), channel_id=1, source_target_pairs={{0,1},{1,0},{2,3},{3,2},{4,5},{5,4},{6,7},{7,6},{8,9},{9,8},{10,11... | collective-permute-start | bytes 1572872 | tf_op jit(solution)/shard_map/ppermute | solution.py:294
  142.8 15.8 %copy-start.16 = (f32[4,4,32,256]{3,2,1,0:T(8,128)S(1)}, f32[4,4,32,256]{3,2,1,0:T(8,128)}, u32[]{:S(2)}) copy-start(f32[4,4,32,256]{3,2,1,0:T(8,128)} %copy-done.15) | copy-start | bytes 1572868
  152.3 6.2 %collective-permute-start.9 = (f32[2,4,128,256]{3,2,1,0:T(8,128)S(1)}, f32[2,4,128,256]{3,2,1,0:T(8,128)S(1)}, u32[]{:S(2)}, u32[]{:S(2)}) collective-permute-start(f32[2,4,128,256]{3,2,1,0:T(8,128)S(1)} %get-tuple-element.37.near_ref.far_ref), channel_id=1, source_target_pairs={{0,1},{1,0},{2,3},{3,2},{4,5},{5,4},{6,7},{7,6},{8,9},{9,8},{10,11... | collective-permute-start | bytes 3145736 | tf_op jit(solution)/shard_map/ppermute | solution.py:294
  156.3 10.7 %collective-permute-start.7 = (f32[2,4,128,256]{3,2,1,0:T(8,128)}, f32[2,4,128,256]{3,2,1,0:T(8,128)S(1)}, u32[]{:S(2)}, u32[]{:S(2)}) collective-permute-start(f32[2,4,128,256]{3,2,1,0:T(8,128)} %get-tuple-element.36.after_any.far_ref.near_ref), channel_id=1, source_target_pairs={{1,2},{2,1},{3,4},{4,3},{5,6},{6,5},{9,10},{10,9},{11,12},{12,11},... | collective-permute-start | bytes 3145736 | tf_op jit(solution)/shard_map/ppermute | solution.py:294
  162.9 13.3 %all-to-all-start.7 = ((f32[4,4,32,256]{3,2,1,0:T(8,128)}), f32[4,4,32,256]{3,2,1,0:T(8,128)S(1)}, u32[]{:S(2)}, u32[]{:S(2)}) async-start(f32[4,4,32,256]{3,2,1,0:T(8,128)} %shard_map.83.after_any), calls=%async_computation.7 | async-start | bytes 1048576 | tf_op jit(solution)/shard_map/all_to_all | solution.py:385
  176.2 20.7 %all-to-all-start.6 = ((f32[4,4,32,256]{3,2,1,0:T(8,128)}), f32[4,4,32,256]{3,2,1,0:T(8,128)S(1)}, u32[]{:S(2)}, u32[]{:S(2)}) async-start(f32[4,4,32,256]{3,2,1,0:T(8,128)} %shard_map.84), calls=%async_computation.6 | async-start | bytes 1048576 | tf_op jit(solution)/shard_map/all_to_all | solution.py:385
  (18 other events, 19.1 us)
where the time goes:
time: 200 us; the launch traced here: 198 us
  Pallas kernels  79.6 us (40%)
  starting transfers between devices  49.6 us (25%)
  waiting for transfers between devices  29.3 us (15%)
  local copies, waits for them, and re-layouts  22.5 us (11%)
  blocking collectives  15.3 us (8%)
    pallas_call x4, Pallas kernels, step_half(): call(step_kernel if last else plain_step_kernel, (views,), [SMEM] + [whol...  39.9 us
    all_to_all x8, starting transfers between devices, exchange(): return lax.all_to_all(values, 'view', 0, 0)  33.5 us
    all_to_all x8, waiting for transfers between devices, exchange(): return lax.all_to_all(values, 'view', 0, 0)  27.7 us
    unnamed x64, local copies, waits for them, and re-layouts  22.5 us
    pallas_call x6, Pallas kernels, depth_half(): call(scale_kernel if scale is None else log_kernel, (1,), [SMEM] + [whole...  17.3 us
    ppermute x10, starting transfers between devices, swap(): return lax.ppermute(values, 'depth', pairs)  16.1 us
    psum x1, blocking collectives, body(): divergence = lax.psum(local, 'depth') / voxel_total  15.3 us
    pallas_call x2, Pallas kernels, ones_half(): call(ones_kernel, (views,), [ANY] * 4, field_shape, per_view(field_shape....  8.13 us
  transfers between devices with their start and end apart: 18, of which 7 were waited for; matrix products, arithmetic and copies ran while one was open for 0% of the time, Pallas kernels for 34%

commit v1 on v0

--- a/solution.py
+++ b/solution.py
@@ -194,9 +194,9 @@
     step_kernel(*refs[:15], None, *refs[15:])
 
 
-def depth_adjoint(place_ref, axial_ref, groups, scale_ref, out_ref):
-    views, half = groups[1].shape[:2]
-    quarters, _, span, _ = out_ref.shape
+def depth_adjoint(place_ref, axial_ref, groups, quarters, write):
+    views, half, height, _ = groups[1].shape
+    span = height // quarters
 
     def run(ordered):
         def quarter(q, carry):
@@ -210,7 +210,7 @@
                         term = axial_ref[view, tap] * ordered[plane // half][view, plane % half, at, :]
                         total = term if total is None else total + term
                     product = total if product is None else product * total
-                out_ref[q, z] = 1.0 / product if scale_ref is None else jnp.log(product * scale_ref[q, z])
+                write(q, z, product)
             return carry
 
         lax.fori_loop(0, quarters, quarter, 0)
@@ -227,24 +227,33 @@
 
 
 def scale_kernel(place_ref, axial_ref, halo_ref, near_ref, far_ref, after_any, out_ref):
-    depth_adjoint(place_ref, axial_ref, (halo_ref, near_ref, far_ref), None, out_ref)
-
-
-def log_kernel(place_ref, axial_ref, halo_ref, near_ref, far_ref, scale_ref, after_any, out_ref):
-    depth_adjoint(place_ref, axial_ref, (halo_ref, near_ref, far_ref), scale_ref, out_ref)
+    def store(q, z, product):
+        out_ref[q, z] = 1.0 / product
+
+    depth_adjoint(place_ref, axial_ref, (halo_ref, near_ref, far_ref), out_ref.shape[0], store)
+
+
+def log_kernel(place_ref, axial_ref, halo_ref, near_ref, far_ref, scale_ref, before_any, out_ref):
+    def store(q, z, product):
+        out_ref[q, 0, z] = jnp.log(product * scale_ref[q, z])
+
+    depth_adjoint(place_ref, axial_ref, (halo_ref, near_ref, far_ref), out_ref.shape[0], store)
 
 
 def share_kernel(place_ref, own_ref, copies_ref, current_ref):
-    current_ref[...] = own_ref[0]
-    for q in range(copies_ref.shape[0]):
-        copies_ref[q] = own_ref[0]
-
-
-def corrected(pieces_ref, current_ref, views_total):
-    total = pieces_ref[0]
+    for k in range(2):
+        at = place_ref[0] if k == 0 else 1 - place_ref[0]
+        values = own_ref[at]
+        current_ref[k] = values
+        for q in range(copies_ref.shape[0]):
+            copies_ref[q, k] = values
+
+
+def corrected(pieces_ref, current_ref, k, views_total):
+    total = pieces_ref[0, k]
     for q in range(1, pieces_ref.shape[0]):
-        total = total + pieces_ref[q]
-    return current_ref[...] * jnp.exp(total * (1.0 / views_total))
+        total = total + pieces_ref[q, k]
+    return current_ref[k] * jnp.exp(total * (1.0 / views_total))
 
 
 def whole(shape):
@@ -259,14 +268,18 @@
 SMEM = pl.BlockSpec(memory_space=pltpu.SMEM)
 
 
-def call(kernel, grid, in_specs, out_shape, out_specs, scratch=(), prefetch=1, cost=(0, 0), vmem=16, **more):
+def hbm(values):
+    return pltpu.with_memory_space_constraint(values, pltpu.HBM)
+
+
+def call(kernel, grid, in_specs, out_shape, out_specs, scratch=(), prefetch=1, vmem=16, **more):
     return pl.pallas_call(
         kernel,
         out_shape=out_shape,
         grid_spec=pltpu.PrefetchScalarGridSpec(
             num_scalar_prefetch=prefetch, grid=grid, in_specs=in_specs, out_specs=out_specs, scratch_shapes=list(scratch)),
         compiler_params=pltpu.CompilerParams(vmem_limit_bytes=vmem * 1024 * 1024),
-        cost_estimate=pl.CostEstimate(flops=cost[0], bytes_accessed=cost[1], transcendentals=0),
+        cost_estimate=pl.CostEstimate(flops=1024, bytes_accessed=1024, transcendentals=0),
         **more,
     )
 
@@ -304,16 +317,17 @@
     group_shape = shape(quarters, half, span, breadth)
     field_shape = shape(views, half, height, breadth)
     fidelity_shape = shape(views, 8, breadth)
-    current_shape = shape(half, span, breadth)
-    volume = views * bases * half * height * breadth
+    pair_shape = shape(quarters, 2, half, span, breadth)
 
     x_mat, xt_mat, y_mat, yt_mat, axial, noise, gain = call(
         prepare_kernel, (views,), [SMEM, per_view(lateral_taps.shape), whole(axial_taps.shape)],
-        (x_shape, x_shape, y_shape, yt_shape, shape(*axial_taps.shape), noise_shape, gain_shape),
+        tuple(pltpu.HBM(a.shape, a.dtype) for a in (x_shape, x_shape, y_shape, yt_shape, axial_taps, noise_shape, gain_shape)),
         (per_view(x_shape.shape), per_view(x_shape.shape), per_view(y_shape.shape), per_view(yt_shape.shape),
          whole(axial_taps.shape), whole(noise_shape.shape), per_view(gain_shape.shape)),
-        prefetch=0, cost=(volume, volume),
+        prefetch=0,
     )(lateral_taps, lateral_taps, axial_taps)
+    x_mat, xt_mat, y_mat, yt_mat, noise, gain = (hbm(a) for a in (x_mat, xt_mat, y_mat, yt_mat, noise, gain))
+    weights_in = hbm(voxel_weights)
 
     weights_buf = pltpu.VMEM((views, bases, half, height, breadth), BF16)
     x_buf = pltpu.VMEM(x_shape.shape, BF16)
@@ -324,8 +338,8 @@
     def ones_half(which, after):
         return call(
             ones_kernel, (views,), [ANY] * 4, field_shape, per_view(field_shape.shape),
-            [weights_buf, x_buf, yt_buf, sems, mixed_buf], vmem=20, cost=(2 * volume * (breadth + height), 4 * volume),
-        )(halves[which], voxel_weights, xt_mat, yt_mat, after)
+            [weights_buf, x_buf, yt_buf, sems, mixed_buf], vmem=20,
+        )(halves[which], weights_in, xt_mat, yt_mat, after)
 
     def step_half(which, halo, near, far, after, last):
         out = call(
@@ -336,56 +350,61 @@
             [weights_buf, pltpu.VMEM((views, half, height, breadth), F32), x_buf, x_buf, yt_buf, sems,
              pltpu.VMEM((half, 2 * height, breadth), BF16),
              pltpu.VMEM((bases, half * height, breadth), BF16), mixed_buf],
-            vmem=36, cost=(4 * volume * (breadth + height), 4 * volume),
-        )(halves[which], axial, halo, near, far, noise, gain, y_mat, observed, voxel_weights, x_mat, xt_mat, yt_mat, after)
+            vmem=36,
+        )(halves[which], axial, halo, near, far, noise, gain, y_mat, hbm(observed), weights_in, x_mat, xt_mat, yt_mat, after)
         return out if last else (out, None)
 
-    def depth_half(which, halo, near, far, after, scale=None):
-        scales_in = () if scale is None else (scale,)
+    def scale_half(which, halo, near, far, after):
         return call(
-            scale_kernel if scale is None else log_kernel, (1,),
-            [SMEM] + [whole(field_shape.shape)] * 3 + [whole(group_shape.shape)] * len(scales_in) + [ANY],
-            group_shape, whole(group_shape.shape), cost=(20 * near.size, 16 * near.size),
-        )(halves[which], axial, halo, near, far, *scales_in, after)
-
-    own_block = pl.BlockSpec((1, half, span, breadth), lambda _, place: (place[0], 0, 0, 0))
-    own_cost = half * span * breadth
-
-    def share(which):
+            scale_kernel, (1,), [SMEM] + [whole(field_shape.shape)] * 3 + [ANY], group_shape, whole(group_shape.shape),
+        )(halves[which], axial, halo, near, far, after)
+
+    def log_half(which, halo, near, far, scale, so_far):
+        aliased = so_far is not None
+        block = pl.BlockSpec((quarters, 1, half, span, breadth), lambda *_: (0, which, 0, 0, 0))
+        return call(
+            log_kernel, (1,), [SMEM] + [whole(field_shape.shape)] * 3 + [whole(group_shape.shape), ANY],
+            pltpu.HBM(pair_shape.shape, F32), block, input_output_aliases={6: 0} if aliased else {},
+        )(halves[which], axial, halo, near, far, scale, hbm(so_far) if aliased else axial)
+
+    def share():
         own = estimate.reshape(2, half, span, breadth)
         return call(
-            share_kernel, (1,), [own_block], (group_shape, current_shape),
-            (whole(group_shape.shape), whole(current_shape.shape)), cost=(own_cost, 8 * own_cost),
-        )(halves[which], own)
+            share_kernel, (1,), [whole(own.shape)], (pltpu.HBM(pair_shape.shape, F32), pltpu.HBM(own.shape, F32)),
+            (whole(pair_shape.shape), whole(own.shape)),
+        )(halves[0], own)
 
     def update(pieces, current):
-        def kernel(pieces_ref, current_ref, copies_ref, new_ref):
-            new_ref[...] = corrected(pieces_ref, current_ref, views_total)
-            for q in range(quarters):
-                copies_ref[q] = new_ref[...]
+        def kernel(pieces_ref, current_ref, first_ref, second_ref, new_ref):
+            for k, copies_ref in enumerate((first_ref, second_ref)):
+                new_ref[k] = corrected(pieces_ref, current_ref, k, views_total)
+                for q in range(quarters):
+                    copies_ref[q] = new_ref[k]
+
+        group_hbm = pltpu.HBM(group_shape.shape, F32)
+        *copies, new = call(
+            kernel, (1,), [whole(pair_shape.shape), whole(current.shape)],
+            (group_hbm, group_hbm, pltpu.HBM(current.shape, F32)),
+            (whole(group_shape.shape), whole(group_shape.shape), whole(current.shape)), prefetch=0,
+        )(pieces, hbm(current))
+        return copies, new
+
+    def finish(pieces, current):
+        def kernel(place_ref, pieces_ref, current_ref, out_ref):
+            for k in range(2):
+                at = place_ref[0] if k == 0 else 1 - place_ref[0]
+                out_ref[at] = corrected(pieces_ref, current_ref, k, views_total)
 
         return call(
-            kernel, (1,), [whole(group_shape.shape), whole(current_shape.shape)], (group_shape, current_shape),
-            (whole(group_shape.shape), whole(current_shape.shape)), prefetch=0, cost=(8 * own_cost, 40 * own_cost),
-        )(pieces, current)
-
-    def finish(which, pieces, current, so_far):
-        aliased = so_far is not None
-
-        def kernel(place_ref, pieces_ref, current_ref, *rest):
-            rest[-1][0] = corrected(pieces_ref, current_ref, views_total)
-
-        return call(
-            kernel, (1,), [whole(group_shape.shape), whole(current_shape.shape)] + [ANY] * aliased,
-            shape(2, half, span, breadth), own_block,
-            cost=(8 * own_cost, 24 * own_cost), input_output_aliases={3: 0} if aliased else {},
-        )(halves[which], pieces, current, *((so_far,) if aliased else ()))
+            kernel, (1,), [whole(pair_shape.shape), whole(current.shape)], shape(*current.shape), whole(current.shape),
+        )(halves[0], pieces, hbm(current))
 
     def exchange(values):
         return lax.all_to_all(values, "view", 0, 0)
 
-    copies, current = zip(*[share(k) for k in range(2)])
-    groups = [exchange(copies[k]) for k in range(2)]
+    copies, current = share()
+    gathered = exchange(copies)
+    groups = [gathered[:, k] for k in range(2)]
     sens, sens_halo = [None, None], [None, None]
     for k in range(2):
         sens[k] = ones_half(k, sens[0] if k else axial)
@@ -400,20 +419,16 @@
             fields_halo[k] = swap(fields[k], k)
         if iteration == 0:
             for k in range(2):
-                scales[k] = depth_half(k, sens_halo[k], sens[k], sens[1 - k], scales[0] if k else axial)
-        order = (1, 0) if last else (0, 1)
-        pieces, logs = [None, None], axial
-        for k in order:
-            logs = depth_half(k, fields_halo[k], fields[k], fields[1 - k], logs, scales[k])
-            pieces[k] = exchange(logs)
+                scales[k] = scale_half(k, sens_halo[k], sens[k], sens[1 - k], axial)
+        logs = None
+        for k in range(2):
+            logs = log_half(k, fields_halo[k], fields[k], fields[1 - k], scales[k], logs)
+        pieces = exchange(logs)
         if not last:
-            copies, current = zip(*[update(pieces[k], current[k]) for k in range(2)])
+            copies, current = update(pieces, current)
             groups = [exchange(copies[k]) for k in range(2)]
-    local = jnp.sum(parts[0] + parts[1], axis=(1, 2))
-    updated = finish(order[0], pieces[order[0]], current[order[0]], None)
-    local, updated = lax.optimization_barrier((local, updated))
-    divergence = lax.psum(local, "depth") / voxel_total
-    updated = finish(order[1], pieces[order[1]], current[order[1]], updated)
+    divergence = lax.psum(jnp.sum(parts[0] + parts[1], axis=(1, 2)), "depth") / voxel_total
+    updated = finish(pieces, current)
     return updated.reshape(estimate.shape), divergence
 
 

time: 200 us -> 183 us (0.915)
  blocking collectives: 15.3 us -> 63.2 us
  waiting for transfers between devices: 29.3 us -> 5.87 us
  starting transfers between devices: 49.6 us -> 26.6 us
  local copies, waits for them, and re-layouts: 22.5 us -> 1.66 us
  Pallas kernels: 79.6 us -> 83.3 us
    all_to_all x0 -> x3, blocking collectives: none -> 48.8 us  [exchange(): return lax.all_to_all(values, 'view', 0, 0)]
    all_to_all x8 -> x2, starting transfers between devices: 33.5 us -> 7.62 us  [exchange(): return lax.all_to_all(values, 'view', 0, 0)]
    all_to_all x8 -> x2, waiting for transfers between devices: 27.7 us -> 5.84 us  [exchange(): return lax.all_to_all(values, 'view', 0, 0)]
    unnamed x64 -> x10, local copies, waits for them, and re-layouts: 22.5 us -> 1.56 us
    pallas_call x12 -> x9, Pallas kernels: 24.8 us -> 20.7 us  [the longest x4 10.9 us: log_half(): call(log_kernel, (1,), [SMEM] + [whole(field_shape.shape)] * 3 + [whole(g...]
    pallas_call x4, Pallas kernels: 39.9 us -> 43.6 us  [step_half(): call(step_kernel if last else plain_step_kernel, (views,), [SMEM] + [whol...]
    ppermute x10, starting transfers between devices: 16.1 us -> 19 us  [swap(): return lax.ppermute(values, 'depth', pairs)]
    pallas_call x1, Pallas kernels: 6.83 us -> 8.93 us  [body(): call(prepare_kernel, (views,), [SMEM, per_view(lateral_taps.shape), whole...]
  transfers between devices with their start and end apart: 18 -> 12, of which waited for: 7 -> 1; matrix products, arithmetic and copies ran while one was open for 0% -> 0% of each run, Pallas kernels for 34% -> 39%
where the time goes in v1:
time: 183 us; the launch traced here: 182 us
  Pallas kernels  83.3 us (46%)
  blocking collectives  63.2 us (35%)
  starting transfers between devices  26.6 us (15%)
  waiting for transfers between devices  5.87 us (3%)
    all_to_all x3, blocking collectives, exchange(): return lax.all_to_all(values, 'view', 0, 0)  48.8 us
    pallas_call x4, Pallas kernels, step_half(): call(step_kernel if last else plain_step_kernel, (views,), [SMEM] + [whol...  43.6 us
    ppermute x10, starting transfers between devices, swap(): return lax.ppermute(values, 'depth', pairs)  19 us
    psum x1, blocking collectives, body(): lax.psum(jnp.sum(parts[0] + parts[1], axis=(1, 2)), 'depth') / voxel_total  14.5 us
    pallas_call x4, Pallas kernels, log_half(): call(log_kernel, (1,), [SMEM] + [whole(field_shape.shape)] * 3 + [whole(g...  10.9 us
    pallas_call x2, Pallas kernels, ones_half(): call(ones_kernel, (views,), [ANY] * 4, field_shape, per_view(field_shape....  10.2 us
    pallas_call x1, Pallas kernels, body(): call(prepare_kernel, (views,), [SMEM, per_view(lateral_taps.shape), whole...  8.93 us
    all_to_all x2, starting transfers between devices, exchange(): return lax.all_to_all(values, 'view', 0, 0)  7.62 us
  transfers between devices with their start and end apart: 12, of which 1 were waited for; matrix products, arithmetic and copies ran while one was open for 0% of the time, Pallas kernels for 39%

profile of v1, /device:TPU:0, one launch (start us, length us, event | category | flops | bytes accessed | tf_op | source)
XLA Modules:
  0.0 182.3 jit_solution(1237105951821340869)
XLA Ops:
  0.7 0.9 copy-done.2
  1.7 1.7 shard_map.69
  3.4 19.4 %all_to_all.25 = f32[4,2,4,32,256]{4,3,2,1,0:T(8,128)S(1)} all-to-all(f32[4,2,4,32,256]{4,3,2,1,0:T(8,128)} %get-tuple-element.19), channel_id=1, replica_groups=mesh['view'=4,'depth'=8] {'view'}, dimensions={0} | all-to-all | bytes 2097152 | tf_op jit(solution)/shard_map/all_to_all | solution.py:403
  22.9 0.7 collective-permute-start.1
  23.6 3.0 %collective-permute-start = (f32[4,4,32,256]{3,2,1,0:T(8,128)S(1)}, f32[4,4,32,256]{3,2,1,0:T(8,128)S(1)}, u32[]{:S(2)}, u32[]{:S(2)}) collective-permute-start(f32[4,4,32,256]{3,2,1,0:T(8,128)S(1)} %get-tuple-element.35.refs_4_.refs_3_), channel_id=1, source_target_pairs={{0,1},{1,0},{2,3},{3,2},{4,5},{5,4},{6,7},{7,6},{8,9},{9,8},{10,11... | collective-permute-start | bytes 1572872 | tf_op jit(solution)/shard_map/ppermute | solution.py:307
  26.6 8.9 %shard_map.68 = (bf16[2,8,256,256]{3,2,1,0:T(8,128)(2,1)}, bf16[2,8,256,256]{3,2,1,0:T(8,128)(2,1)}, bf16[2,1024,128]{2,1,0:T(8,128)(2,1)}, bf16[2,128,1024]{2,1...) custom-call(f32[2,8,2,9]{3,2,1,0:T(2,128)S(1)} %copy-done.3, ...), custom_call_target="tpu_custom_call" | custom-call | flops 1024 | bytes 1024 | tf_op jit(solution)/shard_map/pallas_call | solution.py:322
  36.2 5.1 %shard_map.72.after_any.far_ref.near_ref = f32[2,4,128,256]{3,2,1,0:T(8,128)S(1)} custom-call(s32[3]{0:T(128)S(1)} %pad_add_fusion.place_ref.refs_0_, bf16[2,8,8,128,256]{4,3,2,1,0:T(8,128)(2,1)} %weights_any.7, bf16[2,8,256,256]{3,2,1,0:T(8,128)(2,1)} %get-tuple-element.24.refs_11_.xt_any, bf16[2,128,1024]{2,1,0:T(8,128)(2,1)} %get-tuple-element.25.refs_12_.yt_any, ...), custom_call_target="tpu_custom_call" | custom-call | flops 1024 | bytes 1024 | tf_op jit(solution)/shard_map/pallas_call | solution.py:339
  41.3 0.8 collective-permute-start.5
  42.2 5.1 %shard_map.73.near_ref.far_ref = f32[2,4,128,256]{3,2,1,0:T(8,128)S(1)} custom-call(s32[3]{0:T(128)S(1)} %pad_add_fusion.1.refs_0_.place_ref, bf16[2,8,8,128,256]{4,3,2,1,0:T(8,128)(2,1)} %weights_any.7, bf16[2,8,256,256]{3,2,1,0:T(8,128)(2,1)} %get-tuple-element.24.refs_11_.xt_any, bf16[2,128,1024]{2,1,0:T(8,128)(2,1)} %get-tuple-element.25.refs_12_.yt_any, ...), custom_call_target="tpu_custom_call" | custom-call | flops 1024 | bytes 1024 | tf_op jit(solution)/shard_map/pallas_call | solution.py:339
  47.3 2.9 %collective-permute-start.3 = (f32[2,4,128,256]{3,2,1,0:T(8,128)S(1)}, f32[2,4,128,256]{3,2,1,0:T(8,128)S(1)}, u32[]{:S(2)}, u32[]{:S(2)}) collective-permute-start(f32[2,4,128,256]{3,2,1,0:T(8,128)S(1)} %shard_map.73.near_ref.far_ref), channel_id=1, source_target_pairs={{0,1},{1,0},{2,3},{3,2},{4,5},{5,4},{6,7},{7,6},{8,9},{9,8},{10,11... | collective-permute-start | bytes 3145736 | tf_op jit(solution)/shard_map/ppermute | solution.py:307
  50.2 10.8 %shard_map.70.refs_13_.near_ref.far_ref = f32[2,4,128,256]{3,2,1,0:T(8,128)S(1)} custom-call(s32[3]{0:T(128)S(1)} %pad_add_fusion.place_ref.refs_0_, f32[2,9]{1,0:T(2,128)S(1)} %copy-done.1, f32[4,4,32,256]{3,2,1,0:T(8,128)S(1)} %collective-permute-done.1.refs_2_, f32[4,4,32,256]{3,2,1,0:T(8,128)S(1)} %get-tuple-element.34.refs_3_.refs_4_, ...), custom_call_target="tpu_custom_call" | custom-call | flops 1024 | bytes 1024 | tf_op jit(solution)/shard_map/pallas_call | solution.py:345
  61.0 0.9 collective-permute-start.4
  62.0 10.8 %shard_map.71.far_ref.near_ref = f32[2,4,128,256]{3,2,1,0:T(8,128)S(1)} custom-call(s32[3]{0:T(128)S(1)} %pad_add_fusion.1.refs_0_.place_ref, f32[2,9]{1,0:T(2,128)S(1)} %copy-done.1, f32[4,4,32,256]{3,2,1,0:T(8,128)S(1)} %collective-permute-done.refs_2_, f32[4,4,32,256]{3,2,1,0:T(8,128)S(1)} %get-tuple-element.35.refs_4_.refs_3_, ...), custom_call_target="tpu_custom_call" | custom-call | flops 1024 | bytes 1024 | tf_op jit(solution)/shard_map/pallas_call | solution.py:345
  72.8 2.9 %collective-permute-start.2 = (f32[2,4,128,256]{3,2,1,0:T(8,128)S(1)}, f32[2,4,128,256]{3,2,1,0:T(8,128)S(1)}, u32[]{:S(2)}, u32[]{:S(2)}) collective-permute-start(f32[2,4,128,256]{3,2,1,0:T(8,128)S(1)} %shard_map.71.far_ref.near_ref), channel_id=1, source_target_pairs={{0,1},{1,0},{2,3},{3,2},{4,5},{5,4},{6,7},{7,6},{8,9},{9,8},{10,11... | collective-permute-start | bytes 3145736 | tf_op jit(solution)/shard_map/ppermute | solution.py:307
  75.7 1.8 %shard_map.74.scale_ref = f32[4,4,32,256]{3,2,1,0:T(8,128)S(1)} custom-call(s32[3]{0:T(128)S(1)} %pad_add_fusion.1.refs_0_.place_ref, f32[2,9]{1,0:T(2,128)S(1)} %copy-done.1, f32[2,4,128,256]{3,2,1,0:T(8,128)S(1)} %collective-permute-done.3.halo_ref, f32[2,4,128,256]{3,2,1,0:T(8,128)S(1)} %shard_map.73.near_ref.far_ref, ...), custom_call_target="tpu_custom_call" | custom-call | flops 1024 | bytes 1024 | tf_op jit(solution)/shard_map/pallas_call | solution.py:358
  77.6 1.8 %shard_map.75.scale_ref = f32[4,4,32,256]{3,2,1,0:T(8,128)S(1)} custom-call(s32[3]{0:T(128)S(1)} %pad_add_fusion.place_ref.refs_0_, f32[2,9]{1,0:T(2,128)S(1)} %copy-done.1, f32[2,4,128,256]{3,2,1,0:T(8,128)S(1)} %collective-permute-done.5.halo_ref, f32[2,4,128,256]{3,2,1,0:T(8,128)S(1)} %shard_map.72.after_any.far_ref.near_ref, ...), custom_call_target="tpu_custom_call" | custom-call | flops 1024 | bytes 1024 | tf_op jit(solution)/shard_map/pallas_call | solution.py:358
  79.4 2.7 %shard_map.76.before_any = f32[4,2,4,32,256]{4,3,2,1,0:T(8,128)} custom-call(s32[3]{0:T(128)S(1)} %pad_add_fusion.place_ref.refs_0_, f32[2,9]{1,0:T(2,128)S(1)} %copy-done.1, f32[2,4,128,256]{3,2,1,0:T(8,128)S(1)} %collective-permute-done.4.halo_ref, f32[2,4,128,256]{3,2,1,0:T(8,128)S(1)} %shard_map.70.refs_13_.near_ref.far_ref, ...), custom_call_target="tpu_custom_call" | custom-call | flops 1024 | bytes 1024 | tf_op jit(solution)/shard_map/pallas_call | solution.py:365
  82.2 2.7 %shard_map.77 = f32[4,2,4,32,256]{4,3,2,1,0:T(8,128)} custom-call(s32[3]{0:T(128)S(1)} %pad_add_fusion.1.refs_0_.place_ref, f32[2,9]{1,0:T(2,128)S(1)} %copy-done.1, f32[2,4,128,256]{3,2,1,0:T(8,128)S(1)} %collective-permute-done.2.halo_ref, f32[2,4,128,256]{3,2,1,0:T(8,128)S(1)} %shard_map.71.far_ref.near_ref, ...), custom_call_target="tpu_custom_call", output_to_operand_aliasing={{}: (6, {})} | custom-call | flops 1024 | bytes 1024 | tf_op jit(solution)/shard_map/pallas_call | solution.py:365
  84.9 18.1 %all_to_all.26.pieces_ref = f32[4,2,4,32,256]{4,3,2,1,0:T(8,128)S(1)} all-to-all(f32[4,2,4,32,256]{4,3,2,1,0:T(8,128)} %shard_map.77), channel_id=1, replica_groups=mesh['view'=4,'depth'=8] {'view'}, dimensions={0} | all-to-all | bytes 2097152 | tf_op jit(solution)/shard_map/all_to_all | solution.py:403
  103.0 2.2 %shard_map.78 = (f32[4,4,32,256]{3,2,1,0:T(8,128)}, f32[4,4,32,256]{3,2,1,0:T(8,128)}, f32[2,4,32,256]{3,2,1,0:T(8,128)}) custom-call(f32[4,2,4,32,256]{4,3,2,1,0:T(8,128)S(1)} %all_to_all.26.pieces_ref, f32[2,4,32,256]{3,2,1,0:T(8,128)} %get-tuple-element.26.current_ref), custom_call_target="tpu_custom_call" | custom-call | flops 1024 | bytes 1024 | tf_op jit(solution)/shard_map/pallas_call | solution.py:385
  105.1 11.2 %all_to_all.27.near_ref.far_ref = f32[4,4,32,256]{3,2,1,0:T(8,128)S(1)} all-to-all(f32[4,4,32,256]{3,2,1,0:T(8,128)} %get-tuple-element.28), channel_id=1, replica_groups=mesh['view'=4,'depth'=8] {'view'}, dimensions={0} | all-to-all | bytes 1048576 | tf_op jit(solution)/shard_map/all_to_all | solution.py:403
  116.3 3.5 %all-to-all-start.2 = ((f32[4,4,32,256]{3,2,1,0:T(8,128)}), f32[4,4,32,256]{3,2,1,0:T(8,128)S(1)}, u32[]{:S(2)}, u32[]{:S(2)}) async-start(f32[4,4,32,256]{3,2,1,0:T(8,128)} %get-tuple-element.27), calls=%async_computation.2 | async-start | bytes 1048576 | tf_op jit(solution)/shard_map/all_to_all | solution.py:403
  120.5 5.8 %all-to-all-done.2.far_ref.near_ref = f32[4,4,32,256]{3,2,1,0:T(8,128)S(1)} async-done(((f32[4,4,32,256]{3,2,1,0:T(8,128)}), f32[4,4,32,256]{3,2,1,0:T(8,128)S(1)}, u32[]{:S(2)}, u32[]{:S(2)}) %all-to-all-start.2) | async-done | bytes 524320 | tf_op jit(solution)/shard_map/all_to_all | solution.py:403
  126.4 11.0 %shard_map.79 = (f32[2,4,128,256]{3,2,1,0:T(8,128)S(1)}, f32[2,8,256]{2,1,0:T(8,128)S(1)}) custom-call(s32[3]{0:T(128)S(1)} %pad_add_fusion.place_ref.refs_0_, f32[2,9]{1,0:T(2,128)S(1)} %copy-done.1, f32[4,4,32,256]{3,2,1,0:T(8,128)S(1)} %collective-permute-done.7.halo_ref, f32[4,4,32,256]{3,2,1,0:T(8,128)S(1)} %all_to_all.27.near_ref.far_ref, ...), custom_call_target="tpu_custom_call" | custom-call | flops 1024 | bytes 1024 | tf_op jit(solution)/shard_map/pallas_call | solution.py:345
  137.3 0.9 collective-permute-start.9
  138.3 11.0 %shard_map.80 = (f32[2,4,128,256]{3,2,1,0:T(8,128)S(1)}, f32[2,8,256]{2,1,0:T(8,128)S(1)}) custom-call(s32[3]{0:T(128)S(1)} %pad_add_fusion.1.refs_0_.place_ref, f32[2,9]{1,0:T(2,128)S(1)} %copy-done.1, f32[4,4,32,256]{3,2,1,0:T(8,128)S(1)} %collective-permute-done.6.halo_ref, f32[4,4,32,256]{3,2,1,0:T(8,128)S(1)} %all-to-all-done.2.far_ref.near_ref, ...), custom_call_target="tpu_custom_call" | custom-call | flops 1024 | bytes 1024 | tf_op jit(solution)/shard_map/pallas_call | solution.py:345
  149.3 6.0 %collective-permute-start.8 = (f32[2,4,128,256]{3,2,1,0:T(8,128)S(1)}, f32[2,4,128,256]{3,2,1,0:T(8,128)S(1)}, u32[]{:S(2)}, u32[]{:S(2)}) collective-permute-start(f32[2,4,128,256]{3,2,1,0:T(8,128)S(1)} %get-tuple-element.30.far_ref.near_ref), channel_id=1, source_target_pairs={{0,1},{1,0},{2,3},{3,2},{4,5},{5,4},{6,7},{7,6},{8,9},{9,8},{10,11... | collective-permute-start | bytes 3145736 | tf_op jit(solution)/shard_map/ppermute | solution.py:307
  155.4 2.7 %shard_map.81.before_any = f32[4,2,4,32,256]{4,3,2,1,0:T(8,128)} custom-call(s32[3]{0:T(128)S(1)} %pad_add_fusion.place_ref.refs_0_, f32[2,9]{1,0:T(2,128)S(1)} %copy-done.1, f32[2,4,128,256]{3,2,1,0:T(8,128)S(1)} %collective-permute-done.9.halo_ref, f32[2,4,128,256]{3,2,1,0:T(8,128)S(1)} %get-tuple-element.29.after_any.near_ref.far_ref, ...), custom_call_target="tpu_custom_call" | custom-call | flops 1024 | bytes 1024 | tf_op jit(solution)/shard_map/pallas_call | solution.py:365
  158.1 2.7 %shard_map.82 = f32[4,2,4,32,256]{4,3,2,1,0:T(8,128)} custom-call(s32[3]{0:T(128)S(1)} %pad_add_fusion.1.refs_0_.place_ref, f32[2,9]{1,0:T(2,128)S(1)} %copy-done.1, f32[2,4,128,256]{3,2,1,0:T(8,128)S(1)} %collective-permute-done.8.halo_ref, f32[2,4,128,256]{3,2,1,0:T(8,128)S(1)} %get-tuple-element.30.far_ref.near_ref, ...), custom_call_target="tpu_custom_call", output_to_operand_aliasing={{}: (6, {})} | custom-call | flops 1024 | bytes 1024 | tf_op jit(solution)/shard_map/pallas_call | solution.py:365
  160.8 4.2 %all-to-all-start.4 = ((f32[4,2,4,32,256]{4,3,2,1,0:T(8,128)}), f32[4,2,4,32,256]{4,3,2,1,0:T(8,128)S(1)}, u32[]{:S(2)}, u32[]{:S(2)}) async-start(f32[4,2,4,32,256]{4,3,2,1,0:T(8,128)} %shard_map.82), calls=%async_computation.4 | async-start | bytes 2097152 | tf_op jit(solution)/shard_map/all_to_all | solution.py:403
  165.1 14.5 %psum.7 = f32[2]{0:T(128)S(1)} all-reduce(f32[2]{0:T(128)S(1)} %add_reduce_fusion), channel_id=1, replica_groups=mesh['view'=4,'depth'=8] {'depth'}, use_global_device_ids=true, to_apply=%region_1.0 | all-reduce | flops 2 | bytes 16 | tf_op jit(solution)/shard_map/psum | solution.py:430
  180.0 2.3 %shard_map.83 = f32[2,4,32,256]{3,2,1,0:T(8,128)} custom-call(s32[3]{0:T(128)S(1)} %pad_add_fusion.place_ref.refs_0_, f32[4,2,4,32,256]{4,3,2,1,0:T(8,128)S(1)} %all-to-all-done.4.pieces_ref, f32[2,4,32,256]{3,2,1,0:T(8,128)} %get-tuple-element.31.current_ref), custom_call_target="tpu_custom_call" | custom-call | flops 1024 | bytes 1024 | tf_op jit(solution)/shard_map/pallas_call | solution.py:398
  (27 shorter events, 2.2 us)
Async XLA Ops:
  0.7 1.0 copy-start.2
  3.4 23.3 %copy-start.3 = (f32[2,8,2,9]{3,2,1,0:T(2,128)S(1)}, f32[2,8,2,9]{3,2,1,0:T(2,128)}, u32[]{:S(2)}) copy-start(f32[2,8,2,9]{3,2,1,0:T(2,128)} %lateral_ref.1) | copy-start | bytes 3460
  3.4 23.3 %copy-start.4 = (f32[2,9]{1,0:T(2,128)S(1)}, f32[2,9]{1,0:T(2,128)}, u32[]{:S(2)}) copy-start(f32[2,9]{1,0:T(2,128)} %axial_ref.1) | copy-start | bytes 220
  22.9 27.3 %collective-permute-start.1 = (f32[4,4,32,256]{3,2,1,0:T(8,128)S(1)}, f32[4,4,32,256]{3,2,1,0:T(8,128)S(1)}, u32[]{:S(2)}, u32[]{:S(2)}) collective-permute-start(f32[4,4,32,256]{3,2,1,0:T(8,128)S(1)} %get-tuple-element.34.refs_3_.refs_4_), channel_id=1, source_target_pairs={{1,2},{2,1},{3,4},{4,3},{5,6},{6,5},{9,10},{10,9},{11,12},{12,11},... | collective-permute-start | bytes 1572872 | tf_op jit(solution)/shard_map/ppermute | solution.py:307
  23.6 38.3 %collective-permute-start = (f32[4,4,32,256]{3,2,1,0:T(8,128)S(1)}, f32[4,4,32,256]{3,2,1,0:T(8,128)S(1)}, u32[]{:S(2)}, u32[]{:S(2)}) collective-permute-start(f32[4,4,32,256]{3,2,1,0:T(8,128)S(1)} %get-tuple-element.35.refs_4_.refs_3_), channel_id=1, source_target_pairs={{0,1},{1,0},{2,3},{3,2},{4,5},{5,4},{6,7},{7,6},{8,9},{9,8},{10,11... | collective-permute-start | bytes 1572872 | tf_op jit(solution)/shard_map/ppermute | solution.py:307
  35.6 0.6 copy-start
  41.3 8.9 %copy-start.1 = (f32[2,9]{1,0:T(2,128)S(1)}, f32[2,9]{1,0:T(2,128)}, u32[]{:S(2)}) copy-start(f32[2,9]{1,0:T(2,128)} %get-tuple-element.18.refs_1_.refs_13_.after_any.axial_ref.before_any) | copy-start | bytes 220
  41.3 36.2 %collective-permute-start.5 = (f32[2,4,128,256]{3,2,1,0:T(8,128)S(1)}, f32[2,4,128,256]{3,2,1,0:T(8,128)S(1)}, u32[]{:S(2)}, u32[]{:S(2)}) collective-permute-start(f32[2,4,128,256]{3,2,1,0:T(8,128)S(1)} %shard_map.72.after_any.far_ref.near_ref), channel_id=1, source_target_pairs={{1,2},{2,1},{3,4},{4,3},{5,6},{6,5},{9,10},{10,9},{11,12},{12,11},... | collective-permute-start | bytes 3145736 | tf_op jit(solution)/shard_map/ppermute | solution.py:307
  47.3 28.4 %collective-permute-start.3 = (f32[2,4,128,256]{3,2,1,0:T(8,128)S(1)}, f32[2,4,128,256]{3,2,1,0:T(8,128)S(1)}, u32[]{:S(2)}, u32[]{:S(2)}) collective-permute-start(f32[2,4,128,256]{3,2,1,0:T(8,128)S(1)} %shard_map.73.near_ref.far_ref), channel_id=1, source_target_pairs={{0,1},{1,0},{2,3},{3,2},{4,5},{5,4},{6,7},{7,6},{8,9},{9,8},{10,11... | collective-permute-start | bytes 3145736 | tf_op jit(solution)/shard_map/ppermute | solution.py:307
  61.0 18.4 %collective-permute-start.4 = (f32[2,4,128,256]{3,2,1,0:T(8,128)S(1)}, f32[2,4,128,256]{3,2,1,0:T(8,128)S(1)}, u32[]{:S(2)}, u32[]{:S(2)}) collective-permute-start(f32[2,4,128,256]{3,2,1,0:T(8,128)S(1)} %shard_map.70.refs_13_.near_ref.far_ref), channel_id=1, source_target_pairs={{1,2},{2,1},{3,4},{4,3},{5,6},{6,5},{9,10},{10,9},{11,12},{12,11},... | collective-permute-start | bytes 3145736 | tf_op jit(solution)/shard_map/ppermute | solution.py:307
  72.8 9.4 %collective-permute-start.2 = (f32[2,4,128,256]{3,2,1,0:T(8,128)S(1)}, f32[2,4,128,256]{3,2,1,0:T(8,128)S(1)}, u32[]{:S(2)}, u32[]{:S(2)}) collective-permute-start(f32[2,4,128,256]{3,2,1,0:T(8,128)S(1)} %shard_map.71.far_ref.near_ref), channel_id=1, source_target_pairs={{0,1},{1,0},{2,3},{3,2},{4,5},{5,4},{6,7},{7,6},{8,9},{9,8},{10,11... | collective-permute-start | bytes 3145736 | tf_op jit(solution)/shard_map/ppermute | solution.py:307
  116.3 10.0 %all-to-all-start.2 = ((f32[4,4,32,256]{3,2,1,0:T(8,128)}), f32[4,4,32,256]{3,2,1,0:T(8,128)S(1)}, u32[]{:S(2)}, u32[]{:S(2)}) async-start(f32[4,4,32,256]{3,2,1,0:T(8,128)} %get-tuple-element.27), calls=%async_computation.2 | async-start | bytes 1048576 | tf_op jit(solution)/shard_map/all_to_all | solution.py:403
  119.8 6.6 %collective-permute-start.7 = (f32[4,4,32,256]{3,2,1,0:T(8,128)S(1)}, f32[4,4,32,256]{3,2,1,0:T(8,128)S(1)}, u32[]{:S(2)}, u32[]{:S(2)}) collective-permute-start(f32[4,4,32,256]{3,2,1,0:T(8,128)S(1)} %all_to_all.27.near_ref.far_ref), channel_id=1, source_target_pairs={{1,2},{2,1},{3,4},{4,3},{5,6},{6,5},{9,10},{10,9},{11,12},{12,11},... | collective-permute-start | bytes 1572872 | tf_op jit(solution)/shard_map/ppermute | solution.py:307
  126.4 11.9 %collective-permute-start.6 = (f32[4,4,32,256]{3,2,1,0:T(8,128)S(1)}, f32[4,4,32,256]{3,2,1,0:T(8,128)S(1)}, u32[]{:S(2)}, u32[]{:S(2)}) collective-permute-start(f32[4,4,32,256]{3,2,1,0:T(8,128)S(1)} %all-to-all-done.2.far_ref.near_ref), channel_id=1, source_target_pairs={{0,1},{1,0},{2,3},{3,2},{4,5},{5,4},{6,7},{7,6},{8,9},{9,8},{10,11... | collective-permute-start | bytes 1572872 | tf_op jit(solution)/shard_map/ppermute | solution.py:307
  137.3 18.0 %collective-permute-start.9 = (f32[2,4,128,256]{3,2,1,0:T(8,128)S(1)}, f32[2,4,128,256]{3,2,1,0:T(8,128)S(1)}, u32[]{:S(2)}, u32[]{:S(2)}) collective-permute-start(f32[2,4,128,256]{3,2,1,0:T(8,128)S(1)} %get-tuple-element.29.after_any.near_ref.far_ref), channel_id=1, source_target_pairs={{1,2},{2,1},{3,4},{4,3},{5,6},{6,5},{9,10},{10,9},{11,12},{12,11},... | collective-permute-start | bytes 3145736 | tf_op jit(solution)/shard_map/ppermute | solution.py:307
  149.3 8.7 %collective-permute-start.8 = (f32[2,4,128,256]{3,2,1,0:T(8,128)S(1)}, f32[2,4,128,256]{3,2,1,0:T(8,128)S(1)}, u32[]{:S(2)}, u32[]{:S(2)}) collective-permute-start(f32[2,4,128,256]{3,2,1,0:T(8,128)S(1)} %get-tuple-element.30.far_ref.near_ref), channel_id=1, source_target_pairs={{0,1},{1,0},{2,3},{3,2},{4,5},{5,4},{6,7},{7,6},{8,9},{9,8},{10,11... | collective-permute-start | bytes 3145736 | tf_op jit(solution)/shard_map/ppermute | solution.py:307
  160.8 19.2 %all-to-all-start.4 = ((f32[4,2,4,32,256]{4,3,2,1,0:T(8,128)}), f32[4,2,4,32,256]{4,3,2,1,0:T(8,128)S(1)}, u32[]{:S(2)}, u32[]{:S(2)}) async-start(f32[4,2,4,32,256]{4,3,2,1,0:T(8,128)} %shard_map.82), calls=%async_computation.4 | async-start | bytes 2097152 | tf_op jit(solution)/shard_map/all_to_all | solution.py:403
